TPU v7x, 32 devices: a whole 2x2x4 slice. The times are simulated.
32 devices in a mesh: grp: 16 (over z, y, core), tp: 2 (over x).
Axes of the slice: x: 2, y: 2, z: 4, core: 2. Of those that a mesh axis runs over, the one named last changes fastest.
Arguments:
- tokens: float32 [8192, 1024], P(('grp', 'tp')), may hold values from -6 to 6
- cotangent: float32 [8192, 1024], P(('grp', 'tp')), may hold values from -6 to 6
- lengths: int32 [16, 4], P('grp'), may hold values from 1 to 384, as said below
- order: int32 [16, 4], P('grp'), may hold values from 0 to 3, each once within a row
- weights: float32 [3072, 64, 64], P(('tp', 'grp'))
- momentum: float32 [3072, 64, 64], P(('tp', 'grp')), may hold values from -1.75 to 1.75
- stat_left: float32 [3072, 64, 64], P(('tp', 'grp'))
- stat_right: float32 [3072, 64, 64], P(('tp', 'grp'))
- root_left: float32 [3072, 64, 64], P(('tp', 'grp'))
- root_right: float32 [3072, 64, 64], P(('tp', 'grp'))
- vec_params: float32 [12, 1024], replicated
- vec_momentum: float32 [12, 1024], replicated, may hold values from -3 to 3
- vec_second: float32 [12, 1024], replicated, may hold values from 0.1 to 0.5
Outputs:
- mixed: float32 [8192, 1024], P(('grp', 'tp'))
- input_grad: float32 [8192, 1024], P(('grp', 'tp'))
- weight_grads: float32 [3072, 64, 64], P(('tp', 'grp'))
- stat_left_new: float32 [3072, 64, 64], P(('tp', 'grp'))
- stat_right_new: float32 [3072, 64, 64], P(('tp', 'grp'))
- momentum_new: float32 [3072, 64, 64], P(('tp', 'grp'))
- weights_new: float32 [3072, 64, 64], P(('tp', 'grp'))
- vec_grads: float32 [12, 1024], replicated
- vec_second_new: float32 [12, 1024], replicated
- vec_momentum_new: float32 [12, 1024], replicated
- vec_new: float32 [12, 1024], replicated
Inputs may be any that keep to these rules, and one draw needn't show every extreme that they name: `lengths`: packed in their order, each group's articles fill at most 512 positions, and one article of every group is longer than 256.
All inputs are finite; a program needn't handle non-finite values.
Results may differ from a plain program's by a relative error of at most 0.017.
Values may be sent and summed in bfloat16 or wider, within the bound.
A program may use at most 192 MiB of HBM per device.

v0:
```python
import functools

import jax
import jax.numpy as jnp
from jax import lax
from jax.experimental import pallas as pl
from jax.experimental.pallas import tpu as pltpu
from jax.sharding import PartitionSpec as P

D = 1024
HEADS = 8
HD = 128
FF = 4096
BLOCK = 64


EPS = 1e-05
NEG = -1e30
DECAY = 0.9
BETA = 0.9
RATE = 0.05
VEC_DECAY = 0.9
VEC_RATE = 0.2
VEC_EPS = 1e-08


def norm_rows(value, gain, shift):
    average = jnp.mean(value, -1, keepdims=True)
    centred = value - average
    inverse = lax.rsqrt(jnp.mean(centred * centred, -1, keepdims=True) + EPS)
    normed = centred * inverse
    return (normed * gain + shift, normed, inverse)


def norm_back(grad_out, normed, inverse, gain):
    scaled = grad_out * gain
    return inverse * (
        scaled
        - jnp.mean(scaled, -1, keepdims=True)
        - normed * jnp.mean(scaled * normed, -1, keepdims=True)
    )


def segment_ids(lengths_row, order_row, group_rows):
    article_count = lengths_row.shape[0]
    slots = jnp.arange(article_count, dtype=jnp.int32)
    picks = (order_row[:, None] == slots[None, :]).astype(jnp.int32)
    packed = jnp.sum(picks * lengths_row[None, :], 1)
    ends = jnp.cumsum(packed)
    spots = jnp.arange(group_rows, dtype=jnp.int32)
    return jnp.sum((spots[:, None] >= ends[None, :]).astype(jnp.int32), 1)


def allowed_mask(row_ids, row_segs, segments, key_ids, article_count):
    causal = key_ids[None, :] <= row_ids[:, None]
    same = segments[None, :] == row_segs[:, None]
    alone = (row_segs[:, None] < article_count) | (key_ids[None, :] == row_ids[:, None])
    return causal & same & alone


def from_columns(tiles, row_total, col_total):
    return (
        tiles.reshape(col_total // BLOCK, row_total // BLOCK, BLOCK, BLOCK)
        .transpose(1, 2, 0, 3)
        .reshape(row_total, col_total)
    )


def from_rows(tiles, row_total, col_total):
    return (
        tiles.reshape(row_total // BLOCK, col_total // BLOCK, BLOCK, BLOCK)
        .transpose(0, 2, 1, 3)
        .reshape(row_total, col_total)
    )


def to_columns(matrix):
    row_total, col_total = matrix.shape
    return (
        matrix.reshape(row_total // BLOCK, BLOCK, col_total // BLOCK, BLOCK)
        .transpose(2, 0, 1, 3)
        .reshape(-1, BLOCK, BLOCK)
    )


def to_rows(matrix):
    row_total, col_total = matrix.shape
    return (
        matrix.reshape(row_total // BLOCK, BLOCK, col_total // BLOCK, BLOCK)
        .transpose(0, 2, 1, 3)
        .reshape(-1, BLOCK, BLOCK)
    )


def per_device_general(
    tokens,
    cotangent,
    lengths,
    order,
    weights,
    momentum,
    stat_left,
    stat_right,
    root_left,
    root_right,
    vec_params,
    vec_momentum,
    vec_second,
):
    groups = lax.axis_size("grp")
    tp_size = lax.axis_size("tp")
    tp_rank = lax.axis_index("tp")
    tok_rows = tokens.shape[0]
    group_rows = tok_rows * tp_size
    article_count = lengths.shape[1]
    owners = groups * tp_size
    block_area = BLOCK * BLOCK * owners
    qkv_count = 3 * D * D // block_area
    out_count = D * D // block_area
    in_count = D * FF // block_area
    owned_blocks = weights.shape[0]
    heads_here = HEADS // tp_size
    qkv_cols = 3 * D // tp_size
    feat_here = D // tp_size
    ff_here = FF // tp_size
    qv_width = 2 * D // tp_size
    token_total = group_rows * groups
    gathered = lax.all_gather(weights.astype(jnp.bfloat16), "grp", axis=0, tiled=True)
    per_owner = gathered.reshape(groups, owned_blocks, BLOCK, BLOCK)
    marks = [0, qkv_count, qkv_count + out_count, qkv_count + out_count + in_count, owned_blocks]
    pieces = [
        per_owner[:, marks[index] : marks[index + 1]].reshape(-1, BLOCK, BLOCK)
        for index in range(4)
    ]
    w_qkv = from_columns(pieces[0], D, qkv_cols)
    w_out = from_rows(pieces[1], feat_here, D)
    w_in = from_columns(pieces[2], D, ff_here)
    w_down = from_rows(pieces[3], ff_here, D)
    w_qkv_heads = w_qkv.reshape(D, heads_here, 3, HD)
    w_out_heads = w_out.reshape(heads_here, HD, D)
    segments = segment_ids(lengths[0], order[0], group_rows)
    gain_one = vec_params[0]
    shift_one = vec_params[1]
    gain_two = vec_params[2]
    shift_two = vec_params[3]
    bias_out = vec_params[4]
    bias_down = vec_params[5]
    qv_here = lax.dynamic_slice_in_dim(
        vec_params[6:8].reshape(2 * D), tp_rank * qv_width, qv_width
    ).reshape(heads_here, 2, HD)
    bias_heads = jnp.stack(
        [qv_here[:, 0], jnp.zeros((heads_here, HD), jnp.float32), qv_here[:, 1]], 0
    )[:, :, None, :]
    bias_in = lax.dynamic_slice_in_dim(vec_params[8:].reshape(FF), tp_rank * ff_here, ff_here)
    normed_one, unit_one, inverse_one = norm_rows(tokens, gain_one, shift_one)
    rows_one = lax.all_gather(normed_one.astype(jnp.bfloat16), "tp", axis=0, tiled=True)
    projected = (
        jnp.einsum("rx,xhcd->chrd", rows_one, w_qkv_heads, preferred_element_type=jnp.float32)
        + bias_heads
    ).astype(jnp.bfloat16)
    queries = projected[0]
    keys_all = projected[1]
    values_all = projected[2]
    span = min(512, group_rows)
    starts = jnp.arange(group_rows // span, dtype=jnp.int32) * span
    key_ids = jnp.arange(group_rows, dtype=jnp.int32)
    score_scale = HD ** (-0.5)

    def masked_scores(first_row):
        row_ids = first_row + jnp.arange(span, dtype=jnp.int32)
        row_segs = lax.dynamic_slice_in_dim(segments, first_row, span, 0)
        allowed = allowed_mask(row_ids, row_segs, segments, key_ids, article_count)
        query_rows = lax.dynamic_slice_in_dim(queries, first_row, span, 1)
        scores = (
            jnp.einsum("hqd,hkd->hqk", query_rows, keys_all, preferred_element_type=jnp.float32)
            * score_scale
        )
        return (jnp.where(allowed[None], scores, NEG), query_rows)

    def attend(context_buf, first_row):
        scores, query_rows = masked_scores(first_row)
        row_max = jnp.max(scores, -1, keepdims=True)
        expo = jnp.exp(scores - row_max)
        expsum = jnp.sum(expo, -1, keepdims=True)
        probs_low = (expo / expsum).astype(jnp.bfloat16)
        context = jnp.einsum(
            "hqk,hkd->hqd", probs_low, values_all, preferred_element_type=jnp.float32
        ).astype(jnp.bfloat16)
        context_buf = lax.dynamic_update_slice_in_dim(context_buf, context, first_row, 1)
        return (context_buf, (row_max + jnp.log(expsum))[:, :, 0])

    context_low, log_norm = lax.scan(
        attend, jnp.zeros((heads_here, group_rows, HD), jnp.bfloat16), starts
    )
    attn_sum = lax.psum_scatter(
        jnp.einsum(
            "hrd,hde->re", context_low, w_out_heads, preferred_element_type=jnp.float32
        ).astype(jnp.bfloat16),
        "tp",
        scatter_dimension=0,
        tiled=True,
    ).astype(jnp.float32)
    hidden = tokens + attn_sum + bias_out
    normed_two, unit_two, inverse_two = norm_rows(hidden, gain_two, shift_two)
    rows_two = lax.all_gather(normed_two.astype(jnp.bfloat16), "tp", axis=0, tiled=True)
    inner = jnp.dot(rows_two, w_in, preferred_element_type=jnp.float32) + bias_in
    activ, gelu_pull = jax.vjp(jax.nn.gelu, inner)
    activ_low = activ.astype(jnp.bfloat16)
    mixed = (
        hidden
        + lax.psum_scatter(
            jnp.dot(activ_low, w_down, preferred_element_type=jnp.float32).astype(jnp.bfloat16),
            "tp",
            scatter_dimension=0,
            tiled=True,
        ).astype(jnp.float32)
        + bias_down
    )
    grad_low = cotangent.astype(jnp.bfloat16)
    grad_rows = lax.all_gather(grad_low, "tp", axis=0, tiled=True)
    g_down = jnp.einsum("rf,rd->fd", activ_low, grad_rows, preferred_element_type=jnp.float32)
    grad_activ = jnp.einsum("rd,fd->rf", grad_rows, w_down, preferred_element_type=jnp.float32)
    grad_inner = gelu_pull(grad_activ)[0].astype(jnp.bfloat16)
    g_in = jnp.einsum("rd,rf->df", rows_two, grad_inner, preferred_element_type=jnp.float32)
    g_bias_in = jnp.sum(grad_inner.astype(jnp.float32), 0)
    ffn_blocks = jnp.concatenate(
        [
            to_columns(g_in).reshape(groups, in_count, BLOCK, BLOCK),
            to_rows(g_down).reshape(groups, in_count, BLOCK, BLOCK),
        ],
        1,
    )
    grad_normed_two = lax.psum_scatter(
        jnp.einsum("rf,df->rd", grad_inner, w_in, preferred_element_type=jnp.float32).astype(
            jnp.bfloat16
        ),
        "tp",
        scatter_dimension=0,
        tiled=True,
    ).astype(jnp.float32)
    grad_hidden = cotangent + norm_back(grad_normed_two, unit_two, inverse_two, gain_two)
    grad_attn_low = grad_hidden.astype(jnp.bfloat16)
    grad_attn_rows = lax.all_gather(grad_attn_low, "tp", axis=0, tiled=True)
    g_out = jnp.einsum(
        "hrd,re->hde", context_low, grad_attn_rows, preferred_element_type=jnp.float32
    ).reshape(feat_here, D)
    grad_context = jnp.einsum(
        "re,hde->hrd", grad_attn_rows, w_out_heads, preferred_element_type=jnp.float32
    ).astype(jnp.bfloat16)
    zero_heads = jnp.zeros((heads_here, group_rows, HD), jnp.float32)

    def attend_back(carry, inputs):
        grad_queries, grad_keys, grad_values = carry
        first_row, log_block = inputs
        scores, query_rows = masked_scores(first_row)
        probs = jnp.exp(scores - log_block[:, :, None])
        grad_ctx_rows = lax.dynamic_slice_in_dim(grad_context, first_row, span, 1)
        grad_probs = jnp.einsum(
            "hqd,hkd->hqk", grad_ctx_rows, values_all, preferred_element_type=jnp.float32
        )
        delta = jnp.sum(probs * grad_probs, -1, keepdims=True)
        grad_scores = (probs * (grad_probs - delta)).astype(jnp.bfloat16)
        query_part = (
            jnp.einsum("hqk,hkd->hqd", grad_scores, keys_all, preferred_element_type=jnp.float32)
            * score_scale
        )
        grad_queries = lax.dynamic_update_slice_in_dim(grad_queries, query_part, first_row, 1)
        grad_keys = (
            grad_keys
            + jnp.einsum(
                "hqk,hqd->hkd", grad_scores, query_rows, preferred_element_type=jnp.float32
            )
            * score_scale
        )
        grad_values = grad_values + jnp.einsum(
            "hqk,hqd->hkd",
            probs.astype(jnp.bfloat16),
            grad_ctx_rows,
            preferred_element_type=jnp.float32,
        )
        return ((grad_queries, grad_keys, grad_values), None)

    (grad_queries, grad_keys, grad_values), unused = lax.scan(
        attend_back, (zero_heads, zero_heads, zero_heads), (starts, log_norm)
    )
    grad_proj = jnp.stack([grad_queries, grad_keys, grad_values], 0).astype(jnp.bfloat16)
    proj_sums = jnp.sum(grad_proj.astype(jnp.float32), 2)
    g_bias_qv = jnp.stack([proj_sums[0], proj_sums[2]], 1).reshape(qv_width)
    g_qkv = jnp.einsum(
        "rx,chrd->xhcd", rows_one, grad_proj, preferred_element_type=jnp.float32
    ).reshape(D, qkv_cols)
    grad_normed_one = lax.psum_scatter(
        jnp.einsum(
            "chrd,xhcd->rx", grad_proj, w_qkv_heads, preferred_element_type=jnp.float32
        ).astype(jnp.bfloat16),
        "tp",
        scatter_dimension=0,
        tiled=True,
    ).astype(jnp.float32)
    input_grad = grad_hidden + norm_back(grad_normed_one, unit_one, inverse_one, gain_one)
    local_rows = jnp.stack(
        [
            jnp.sum(grad_normed_one * unit_one, 0),
            jnp.sum(grad_normed_one, 0),
            jnp.sum(grad_normed_two * unit_two, 0),
            jnp.sum(grad_normed_two, 0),
            jnp.sum(grad_hidden, 0),
            jnp.sum(cotangent, 0),
        ]
    )
    qv_rows = lax.dynamic_update_slice(
        jnp.zeros((2 * D,), jnp.float32), g_bias_qv, (tp_rank * qv_width,)
    ).reshape(2, D)
    in_rows = lax.dynamic_update_slice(
        jnp.zeros((FF,), jnp.float32), g_bias_in, (tp_rank * ff_here,)
    ).reshape(FF // D, D)
    vec_grads = lax.psum(jnp.concatenate([local_rows, qv_rows, in_rows], 0), ("grp", "tp"))
    attn_blocks = jnp.concatenate(
        [
            to_columns(g_qkv).reshape(groups, qkv_count, BLOCK, BLOCK),
            to_rows(g_out).reshape(groups, out_count, BLOCK, BLOCK),
        ],
        1,
    )
    every_block = jnp.concatenate([attn_blocks, ffn_blocks], 1).reshape(-1, BLOCK, BLOCK)
    weight_grads = lax.psum_scatter(
        every_block.astype(jnp.bfloat16), "grp", scatter_dimension=0, tiled=True
    ).astype(jnp.float32)
    scaled = weight_grads * token_total ** (-0.5)
    stat_left_new = DECAY * stat_left + (1.0 - DECAY) * jnp.einsum(
        "nij,nkj->nik", scaled, scaled, precision=lax.Precision.HIGHEST
    )
    stat_right_new = DECAY * stat_right + (1.0 - DECAY) * jnp.einsum(
        "nji,njk->nik", scaled, scaled, precision=lax.Precision.HIGHEST
    )
    shaped = jnp.einsum("nij,njk->nik", root_left, scaled, precision=lax.Precision.HIGHEST)
    shaped = jnp.einsum("nij,njk->nik", shaped, root_right, precision=lax.Precision.HIGHEST)
    momentum_new = BETA * momentum + shaped
    weights_new = weights - RATE * momentum_new
    vec_scaled = vec_grads * token_total ** (-0.5)
    vec_second_new = VEC_DECAY * vec_second + (1.0 - VEC_DECAY) * vec_scaled * vec_scaled
    vec_momentum_new = BETA * vec_momentum + vec_scaled * lax.rsqrt(vec_second_new + VEC_EPS)
    vec_new = vec_params - VEC_RATE * vec_momentum_new
    return (
        mixed,
        input_grad,
        weight_grads,
        stat_left_new,
        stat_right_new,
        momentum_new,
        weights_new,
        vec_grads,
        vec_second_new,
        vec_momentum_new,
        vec_new,
    )


MESH_ID = pl.DeviceIdType.MESH
LANES = 128
HALF = 64
VMEM_LIMIT = 62 * 2**20
ARTICLES = 4
GELU_A = (2.0 / 3.141592653589793) ** 0.5
GELU_B = 0.044715


def remote(src, dst, send_sem, recv_sem, device):
    return pltpu.make_async_remote_copy(
        src_ref=src,
        dst_ref=dst,
        send_sem=send_sem,
        recv_sem=recv_sem,
        device_id=device,
        device_id_type=MESH_ID,
    )


def place():
    grp = lax.axis_index("grp")
    return lax.div(grp, 4), lax.rem(lax.div(grp, 2), 2), lax.rem(grp, 2), lax.axis_index("tp")


def slot_of(z, y, c):
    return z * 4 + y * 2 + c


def lay_blocks(view_ref, stack):
    half = view_ref.shape[2] // 2

    def row(i, carry):
        tile = view_ref[i].T
        stack[pl.ds(i, half, stride=BLOCK), :] = jnp.concatenate([tile[:half], tile[half:]], 1)
        return carry

    lax.fori_loop(0, BLOCK, row, 0, unroll=8)


def piece_shapes():
    return ((768, LANES), (64, 512), (1024, LANES), (LANES, 1024))


def both_halves(pair):
    low = lax.broadcasted_iota(jnp.int32, pair.shape, 1) < HALF
    turned = pltpu.roll(pair, HALF, 1)
    return jnp.where(low, pair, turned), jnp.where(low, turned, pair)


def update_kernel(
    scale,
    sum_q,
    sum_o,
    sum_i,
    sum_d,
    root_l,
    root_r,
    vec_g,
    vecs,
    vec_m,
    vec_s,
    mixed,
    input_grad,
    w,
    m,
    sl,
    sr,
    out_g,
    out_sl,
    out_sr,
    out_m,
    out_w,
    out_vg,
    out_vs,
    out_vm,
    out_v,
    out_mixed,
    out_input_grad,
    grads,
    first,
    second,
    held_l,
    held_r,
    held_w,
    held_m,
    held_sl,
    held_sr,
    sems,
    block_sems,
):
    count = w.shape[2]
    step_rows = out_w.shape[0]
    bf, f32 = jnp.bfloat16, jnp.float32

    def loads(k):
        part = pl.ds(16 * k, 16)
        return [
            pltpu.make_async_copy(root.at[part], held.at[part], sems.at[k, side])
            for side, (root, held) in enumerate(((root_l, held_l), (root_r, held_r)))
        ]

    def block_loads(k):
        part = pl.ds(k * step_rows, step_rows)
        pairs = ((w, held_w), (m, held_m), (sl, held_sl), (sr, held_sr))
        return [pltpu.make_async_copy(a.at[part], b.at[part], block_sems.at[k, n]) for n, (a, b) in enumerate(pairs)]

    out_mixed[...] = mixed[...]
    out_input_grad[...] = input_grad[...]

    @pl.when(pl.program_id(0) == 0)
    def _():
        for k in range(4):
            for load in loads(k):
                load.start()
        for k in range(BLOCK // step_rows):
            for load in block_loads(k):
                load.start()
        total = vec_g[...]
        out_vg[...] = total
        scaled = total * scale
        fresh = VEC_DECAY * vec_s[...] + (1.0 - VEC_DECAY) * scaled * scaled
        out_vs[...] = fresh
        momentum = BETA * vec_m[...] + scaled * lax.rsqrt(fresh + VEC_EPS)
        out_vm[...] = momentum
        out_v[...] = vecs[...] - VEC_RATE * momentum
        rows = sum_q.shape[0]
        grads[0:rows, 0:HALF] = sum_q[:, 0:HALF]
        grads[rows : 2 * rows, 0:HALF] = sum_q[:, HALF:LANES]
        base = 2 * rows
        for b in range(8):
            grads[base + b * 64 : base + b * 64 + 64, 0:HALF] = sum_o[:, b * HALF : (b + 1) * HALF]
        base += 512
        grads[base : base + D, 0:HALF] = sum_i[:, 0:HALF]
        grads[0:D, HALF:LANES] = sum_i[:, HALF:LANES]
        for r in range(2):
            for b in range(16):
                at = D + (r * 16 + b) * 64
                grads[at : at + 64, HALF:LANES] = sum_d[r * 64 : r * 64 + 64, b * HALF : (b + 1) * HALF]

        def row(i, carry):
            both = jnp.concatenate([held_l[i], held_r[i]], 0)
            second[pl.ds(i, count, stride=BLOCK), :] = both.T
            return carry

        for k in range(4):
            for load in loads(k):
                load.wait()
            lax.fori_loop(16 * k, 16 * k + 16, row, 0, unroll=8)
        row_id = lax.broadcasted_iota(jnp.int32, (256, 256), 0)
        col_id = lax.broadcasted_iota(jnp.int32, (256, 256), 1)
        mask = lax.shift_right_logical(row_id, 6) == lax.shift_right_logical(col_id, 6)
        low = lax.broadcasted_iota(jnp.int32, (256, LANES), 1) < HALF

        def spread(v):
            return jnp.where(mask, jnp.concatenate([v, v], 1), 0.0).astype(bf)

        def eight(k, carry):
            at = pl.ds(pl.multiple_of(k * 256, 256), 256)
            for side, grad in enumerate(both_halves(grads[at, :])):
                to = pl.ds(pl.multiple_of(k * 256 + side * (count // 2 * BLOCK), 256), 256)
                left, right = both_halves(second[to, :])
                s32 = grad * scale
                s = s32.astype(bf)
                outer = lax.dot_general(s[:, 0:HALF], s[:, 0:HALF], (((1,), (1,)), ((), ())), preferred_element_type=f32)
                kept = jnp.where(mask, outer, 0.0)
                kept = kept[:, :LANES] + kept[:, LANES:]
                outer = kept + pltpu.roll(kept, HALF, 1)
                inner = lax.dot_general(spread(s32), s, (((0,), (0,)), ((), ())), preferred_element_type=f32)
                shaped = jnp.dot(spread(left), s, preferred_element_type=f32)
                shaped = jnp.dot(spread(shaped), right.astype(bf), preferred_element_type=f32)
                first[to, :] = jnp.where(low, grad, outer)
                second[to, :] = jnp.where(low, inner, shaped)
            return carry

        lax.fori_loop(0, count // 8, eight, 0, unroll=4)

    i0 = pl.program_id(0) * step_rows
    for load in block_loads(pl.program_id(0)):
        load.wait()
    unit = lax.broadcasted_iota(jnp.int32, (LANES, LANES), 0) == lax.broadcasted_iota(jnp.int32, (LANES, LANES), 1)
    unit = unit.astype(f32).astype(bf)

    def turned(tile):
        high = tile.astype(bf)
        rest = (tile - high.astype(f32)).astype(bf)
        over = (((1,), (1,)), ((), ()))
        return lax.dot_general(unit, high, over, preferred_element_type=f32) + lax.dot_general(
            unit, rest, over, preferred_element_type=f32
        )


    def rows_out(ii, carry):
        i = i0 + ii
        at = pl.ds(i, count, stride=BLOCK)
        one = first[at, :].T
        two = turned(second[at, :])
        out_g[ii] = one[0:HALF]
        out_sl[ii] = DECAY * held_sl[i] + (1.0 - DECAY) * one[HALF:LANES]
        out_sr[ii] = DECAY * held_sr[i] + (1.0 - DECAY) * two[0:HALF]
        fresh = BETA * held_m[i] + two[HALF:LANES]
        out_m[ii] = fresh
        out_w[ii] = held_w[i] - RATE * fresh
        return carry

    lax.fori_loop(0, step_rows, rows_out, 0, unroll=True)


def update_blocks(sums, blocks, vec_grads, vecs, results, token_total):
    views = [jnp.transpose(a, (1, 2, 0)) for a in blocks]
    count = blocks[0].shape[0]
    rows = 8
    whole = pl.BlockSpec(memory_space=pltpu.VMEM)
    steps = BLOCK // rows
    some = pl.BlockSpec((results[0].shape[0] // steps, results[0].shape[1]), lambda i: (i, 0))
    there = pl.BlockSpec(memory_space=pl.ANY)
    part = pl.BlockSpec((rows, BLOCK, count), lambda i: (i, 0, 0))
    vec = jax.ShapeDtypeStruct(vec_grads.shape, jnp.float32)
    outs = pl.pallas_call(
        functools.partial(update_kernel, token_total ** (-0.5)),
        grid=(steps,),
        out_shape=[jax.ShapeDtypeStruct((BLOCK, BLOCK, count), jnp.float32)] * 5
        + [vec] * 4
        + [jax.ShapeDtypeStruct(a.shape, a.dtype) for a in results],
        in_specs=[whole] * 4 + [there] * 2 + [whole] * 4 + [some] * 2 + [there] * 4,
        out_specs=[part] * 5 + [whole] * 4 + [some] * 2,
        scratch_shapes=[
            pltpu.VMEM((count // 2 * BLOCK, LANES), jnp.float32),
            pltpu.VMEM((count * BLOCK, LANES), jnp.float32),
            pltpu.VMEM((count * BLOCK, LANES), jnp.float32),
            *[pltpu.VMEM((BLOCK, BLOCK, count), jnp.float32)] * 6,
            pltpu.SemaphoreType.DMA((4, 2)),
            pltpu.SemaphoreType.DMA((BLOCK // rows, 4)),
        ],
        compiler_params=pltpu.CompilerParams(vmem_limit_bytes=VMEM_LIMIT),
        name="update_blocks",
    )(*sums, *views[4:], vec_grads, *vecs, *results, *views[:4])
    return [jnp.transpose(a, (2, 0, 1)) for a in outs[:5]], outs[5:9], outs[9:]


DEPTH = 4


def layer_kernel(
    lengths,
    order,
    view,
    tokens,
    cot,
    vecs,
    mixed,
    input_grad,
    sum_q,
    sum_o,
    sum_i,
    sum_d,
    vec_grads,
    gq,
    go,
    gi,
    gd,
    wqkv,
    cq,
    co,
    ci,
    cd,
    yq,
    yo,
    yi,
    yd,
    yv,
    zq,
    zo,
    zi,
    zd,
    zv,
    rows_one,
    rows_two,
    rows_t,
    grad_rows,
    grad_attn,
    probs,
    qkv,
    ctx,
    gctx,
    far,
    inx,
    go_x,
    ctx_x,
    macc,
    nacc,
    act,
    gin,
    bias_sum,
    qkv_bias,
    qv_sum,
    vin,
    vout,
    late,
    late_sum,
    late_in,
    recv,
    send_y,
    send_c,
    send_z,
    rc_recv,
    rc_send,
    ry_recv,
    ry_send,
    rz_recv,
    rz_send,
    x_send,
    x_recv,
    v_send,
    v_recv,
    l_send,
    l_recv,
    copy_sem,
):
    bf, f32 = jnp.bfloat16, jnp.float32
    z, y, c, t = place()
    me = slot_of(z, y, c)
    x_peer = (me, 1 - t)
    y_peer = (slot_of(z, 1 - y, c), t)
    c_peer = (slot_of(z, y, 1 - c), t)
    rows = tokens.shape[0]
    own = pl.ds(pl.multiple_of(t * rows, rows), rows)
    other = pl.ds(pl.multiple_of((1 - t) * rows, rows), rows)

    def lanes(start, size, unit):
        return pl.ds(pl.multiple_of(start, unit), size)

    gathered, core_in = (gq, go, gi, gd), (cq, co, ci, cd)
    y_in, z_in = (yq, yo, yi, yd, yv), (zq, zo, zi, zd, zv)
    sums = (sum_q, sum_o, sum_i, sum_d)
    Q, O, I, W, V = range(5)

    def dot(a, b):
        return jnp.dot(a, b, preferred_element_type=f32)

    def dot_nt(a, b):
        return lax.dot_general(a, b, (((1,), (1,)), ((), ())), preferred_element_type=f32)

    def dot_tn(a, b):
        return lax.dot_general(a, b, (((0,), (0,)), ((), ())), preferred_element_type=f32)

    def piece(k, zz, yy, cc):
        if k == O:
            return go.at[zz * 2 + yy, :, pl.ds(pl.multiple_of(cc * 512, 512), 512)]
        return gathered[k].at[slot_of(zz, yy, cc)]

    def near(s):
        return lax.rem(z + (1 - 2 * lax.div(z, 2)) * s + DEPTH, DEPTH)

    def ag_piece(k, zz, yy, cc):
        if k == W:
            return gd.at[slot_of(zz, yy, cc), 0:HALF]
        if k == V:
            return gd.at[slot_of(zz, yy, cc), HALF:LANES]
        return piece(k, zz, yy, cc)

    def ag_copy(k, zz, yy, way):
        src = ag_piece(k, zz, yy, c)
        sem = recv.at[k, slot_of(zz, yy, c)]
        if way == "up":
            return remote(src, src, send_z.at[k, 0, yy * DEPTH + zz], sem, (slot_of(z + 1, y, c), t))
        if way == "down":
            return remote(src, src, send_z.at[k, 1, yy * DEPTH + zz], sem, (slot_of(z - 1, y, c), t))
        if way == "y":
            return remote(src, src, send_y.at[k, zz], sem, y_peer)
        return remote(src, src, send_c.at[k, yy * DEPTH + zz], sem, c_peer)

    def ag_wait(k, zz, yy, cc):
        ref = ag_piece(k, zz, yy, cc)
        remote(ref, ref, send_y.at[k, 0], recv.at[k, slot_of(zz, yy, cc)], y_peer).wait_recv()

    def own_sends_z(k):
        @pl.when(z < DEPTH - 1)
        def _():
            ag_copy(k, z, y, "up").start()

        @pl.when(z > 0)
        def _():
            ag_copy(k, z, y, "down").start()

        ag_copy(k, z, y, "core").start()

    def own_sends_y(k):
        ag_copy(k, z, y, "y").start()

    def z_arrival(kinds, dist):
        @pl.when(z >= dist)
        def _():
            for k in kinds:
                ag_wait(k, z - dist, y, c)

                @pl.when(z < DEPTH - 1)
                def _():
                    ag_copy(k, z - dist, y, "up").start()

                ag_copy(k, z - dist, y, "y").start()
                ag_copy(k, z - dist, y, "core").start()

        @pl.when(z + dist < DEPTH)
        def _():
            for k in kinds:
                ag_wait(k, z + dist, y, c)

                @pl.when(z > 0)
                def _():
                    ag_copy(k, z + dist, y, "down").start()

                ag_copy(k, z + dist, y, "y").start()
                ag_copy(k, z + dist, y, "core").start()

    def y_arrival(kinds, dist):
        def one(zz):
            for k in kinds:
                ag_wait(k, zz, 1 - y, c)
                ag_copy(k, zz, 1 - y, "core").start()

        if dist == 0:
            one(z)
            return

        @pl.when(z >= dist)
        def _():
            one(z - dist)

        @pl.when(z + dist < DEPTH)
        def _():
            one(z + dist)

    def v_forward(zz, yy):
        ag_wait(V, zz, yy, c)

        @pl.when((zz <= z) & (z < DEPTH - 1))
        def _():
            ag_copy(V, zz, yy, "up").start()

        @pl.when((zz >= z) & (z > 0))
        def _():
            ag_copy(V, zz, yy, "down").start()

        ag_copy(V, zz, yy, "core").start()

    def v_arrival(dist):
        for yy in (y, 1 - y):

            @pl.when(z >= dist)
            def _():
                v_forward(z - dist, yy)

            @pl.when(z + dist < DEPTH)
            def _():
                v_forward(z + dist, yy)

    def drain(k, zz, yy):
        ag_copy(k, zz, yy, "core").wait_send()
        if k == V:

            @pl.when((yy == y) & (zz == z))
            def _():
                ag_copy(k, zz, yy, "y").wait_send()

            @pl.when((zz <= z) & (z < DEPTH - 1))
            def _():
                ag_copy(k, zz, yy, "up").wait_send()

            @pl.when((zz >= z) & (z > 0))
            def _():
                ag_copy(k, zz, yy, "down").wait_send()

            return

        @pl.when(yy == y)
        def _():
            ag_copy(k, zz, y, "y").wait_send()

            @pl.when((zz <= z) & (z < DEPTH - 1))
            def _():
                ag_copy(k, zz, y, "up").wait_send()

            @pl.when((zz >= z) & (z > 0))
            def _():
                ag_copy(k, zz, y, "down").wait_send()

    def add(dst, *terms):
        count, width = dst.shape
        step = min(count, 256 * LANES // width)

        def body(i, carry):
            at = pl.ds(pl.multiple_of(i * step, 16), step)
            if len(terms) == 2 and dst.dtype == bf:
                dst[at, :] = terms[0][at, :] + terms[1][at, :]
                return carry
            total = terms[0][at, :].astype(f32)
            for term in terms[1:]:
                total = total + term[at, :].astype(f32)
            dst[at, :] = total.astype(dst.dtype)
            return carry

        lax.fori_loop(0, count // step, body, 0, unroll=2)

    side = lax.div(z, 2)
    end_z, inner_z = 3 * side, 1 + side
    is_end = z == end_z

    def rc_copy(k, zz, yy):
        at = zz * 2 + yy
        return remote(piece(k, zz, yy, 1 - c), core_in[k].at[at], rc_send.at[k, at], rc_recv.at[k, at], c_peer)

    def ry_copy(k, zz):
        if k == V:
            return remote(ag_piece(V, z, 1 - y, c), y_in[V].at[0], ry_send.at[V, 0], ry_recv.at[V, 0], y_peer)
        return remote(ag_piece(k, zz, 1 - y, c), y_in[k].at[zz], ry_send.at[k, zz], ry_recv.at[k, zz], y_peer)

    def z_slot(k, slot, yy):
        return z_in[k].at[slot * 2 + yy if k == V else slot]

    def z_sem(slot, yy):
        return slot * 2 + yy

    def rz_copy(k, s, yy, from_end):
        slot = s - 1 if from_end else {3: 0, 2: 1, 1: 3}[s]
        to = inner_z if from_end else {3: end_z, 2: 3 - end_z, 1: 3 - inner_z}[s]
        sent, landed = rz_send.at[k, (s - 1) * 2 + yy], rz_recv.at[k, z_sem(slot, yy)]
        return remote(ag_piece(k, near(s), yy, c), z_slot(k, slot, yy), sent, landed, (slot_of(to, y, c), t))

    def z_landed(k, slot, yy):
        ref = z_slot(k, slot, yy)
        remote(ref, ref, rz_send.at[k, 0], rz_recv.at[k, z_sem(slot, yy)], y_peer).wait_recv()
        return ref

    def y_landed(k, zz):
        ref = y_in[k].at[0 if k == V else zz]
        remote(ref, ref, ry_send.at[k, 0], ry_recv.at[k, 0 if k == V else zz], y_peer).wait_recv()
        return ref

    def rc_add(k, zz, yy):
        at = zz * 2 + yy
        remote(core_in[k].at[at], core_in[k].at[at], rc_send.at[k, 0], rc_recv.at[k, at], c_peer).wait_recv()
        mine = piece(k, zz, yy, c)
        add(mine, mine, core_in[k].at[at])

        @pl.when(yy != y)
        def _():
            ry_copy(k, zz).start()

    def z_step(k, s, yy, *terms):
        mine = ag_piece(k, near(s), yy, c)
        if terms:
            add(mine, mine, *terms)

        @pl.when(is_end)
        def _():
            rz_copy(k, s, yy, True).start()

        if s == 3:

            @pl.when(jnp.logical_not(is_end))
            def _():
                rz_copy(k, s, yy, False).start()

    def z_merge(k, s, yy):
        @pl.when(jnp.logical_not(is_end))
        def _():
            mine = ag_piece(k, near(s), yy, c)
            add(mine, mine, z_landed(k, s, yy))
            rz_copy(k, s, yy, False).start()

    def ry_add(k, s):
        z_step(k, s, y, y_landed(k, near(s)))

    def ry_merge(k, s):
        z_merge(k, s, y)

    def total_of(k):
        return sum_d.at[(k - W) * HALF : (k - W + 1) * HALF] if k >= W else sums[k]

    def z_total(k, yy, dst, *terms):
        mine = ag_piece(k, z, yy, c)
        first = z_landed(k, 0, yy)

        @pl.when(is_end)
        def _():
            add(dst, mine, first, z_landed(k, 1, yy), *terms)

        @pl.when(jnp.logical_not(is_end))
        def _():
            add(dst, mine, first, z_landed(k, 3, yy), *terms)

    def own_total(k):
        z_total(k, y, total_of(k), y_landed(k, z))

    def v_cross():
        mine = ag_piece(V, z, 1 - y, c)
        z_total(V, 1 - y, mine)
        ry_copy(V, z).start()

    def x_rows(ref, index):
        return remote(ref.at[own], ref.at[own], x_send.at[index], x_recv.at[index], x_peer)

    def x_rows_wait(ref, index):
        remote(ref.at[other], ref.at[other], x_send.at[index], x_recv.at[index], x_peer).wait_recv()

    def x_part(index):
        slot = 1 if index == 2 else 0
        return remote(far.at[slot], inx.at[slot], x_send.at[5 + index], x_recv.at[5 + index], x_peer)

    def by_rows(body, step=64):
        def run(i, carry):
            body(pl.multiple_of(i * step, step), step)
            return carry

        lax.fori_loop(0, rows // step, run, 0)

    def norm(value):
        average = jnp.mean(value, -1, keepdims=True)
        centred = value - average
        inverse = lax.rsqrt(jnp.mean(centred * centred, -1, keepdims=True) + EPS)
        return centred * inverse, inverse

    def norm_grad(grad, unit, inverse, gain):
        scaled = grad * gain
        return inverse * (
            scaled - jnp.mean(scaled, -1, keepdims=True) - unit * jnp.mean(scaled * unit, -1, keepdims=True)
        )

    def x_out():
        half = (slice(None), slice(None), lanes(c * 512, 512, 512))
        return remote(go.at[half], go_x.at[half], x_send.at[4], x_recv.at[4], x_peer)

    def x_out_core(cc):
        half = (slice(None), slice(None), lanes(cc * 512, 512, 512))
        return remote(go_x.at[half], go_x.at[half], x_send.at[9], x_recv.at[9], c_peer)

    def x_grad_context():
        return remote(ctx_x, gctx.at[own], x_send.at[10], x_recv.at[10], x_peer)

    def x_grad_context_wait():
        remote(gctx.at[other], gctx.at[other], x_send.at[10], x_recv.at[10], x_peer).wait_recv()

    stages = (x_peer, c_peer, y_peer)

    def v_copy(stage):
        return remote(vout.at[1 + stage], vin.at[stage], v_send.at[stage], v_recv.at[stage], stages[stage])

    def vz_copy(step):
        peer = (slot_of(lax.rem(z + step, DEPTH), y, c), t)
        return remote(vout.at[4], vin.at[3 + z], v_send.at[2 + step], v_recv.at[3 + z], peer)

    def early_rows(hop):
        if hop == 0:
            vout[1] = vout[0]
        else:
            v_copy(hop - 1).wait_recv()
            vout[1 + hop] = vout[hop] + vin[hop - 1]
        if hop < 3:
            v_copy(hop).start()
        else:
            for step in range(1, DEPTH):
                vz_copy(step).start()
            vin[3 + z] = vout[4]

    def late_turn(turn):
        dx, dy, dc = turn // 4, turn // 2 % 2, turn % 2
        xx, yy, cc = (1 - t if dx else t), (1 - y if dy else y), (1 - c if dc else c)
        return (slot_of(z, yy, cc), xx), xx * 4 + yy * 2 + cc

    def late_copy(turn):
        here = t * 4 + y * 2 + c
        return remote(late, late_in.at[here], l_send.at[turn], l_recv.at[here], late_turn(turn)[0])

    def late_wait(index):
        remote(late_in.at[index], late_in.at[index], l_send.at[0], l_recv.at[index], y_peer).wait_recv()

    def late_z(step):
        peer = (slot_of(lax.rem(z + step, DEPTH), y, c), t)
        return remote(late_sum, late_in.at[8 + z], l_send.at[7 + step], l_recv.at[8 + z], peer)

    barrier = pltpu.get_barrier_semaphore()
    z_peers = [(slot_of(lax.rem(z + step, DEPTH), y, c), t) for step in range(1, DEPTH)]
    everyone = [late_turn(turn)[0] for turn in range(1, 8)] + z_peers
    for device in everyone:
        pl.semaphore_signal(barrier, inc=1, device_id=device, device_id_type=MESH_ID)

    def prepare(held, stack):
        load = pltpu.make_async_copy(view, held, copy_sem.at[0])
        load.start()

        def first_norm(at, step):
            unit, inverse = norm(tokens[pl.ds(at, step), :])
            to = pl.ds(pl.multiple_of(t * rows + at, step), step)
            rows_one[to, :] = (unit * vecs[0:1, :] + vecs[1:2, :]).astype(bf)
            grad_rows[to, :] = cot[pl.ds(at, step), :].astype(bf)

        load.wait()
        lay_blocks(held, stack)

        def pair(left, right, count, left_high=False, right_high=False):
            first, second = stack[left : left + count, :], stack[right : right + count, :]
            first = pltpu.roll(first, HALF, 1) if left_high else first
            second = second if right_high else pltpu.roll(second, HALF, 1)
            lane = lax.broadcasted_iota(jnp.int32, (count, LANES), 1)
            return jnp.where(lane < HALF, first, second).astype(bf)

        n = gq.shape[1]
        gq[me] = pair(0, n, n)
        base = 2 * n
        wide = [pair(base + b * 64, base + b * 64 + 64, 64) for b in range(0, 8, 2)]
        go[z * 2 + y, :, lanes(c * 512, 512, 512)] = jnp.concatenate(wide, 1)
        pl.semaphore_wait(barrier, len(everyone))
        for k in (Q, O):
            own_sends_y(k)
            own_sends_z(k)
        by_rows(first_norm)
        x_rows(rows_one, 0).start()
        base += 512
        gi[me] = pair(base, 0, D, right_high=True)
        for r in range(2):
            for b in range(0, 16, 2):
                at = D + (r * 16 + b) * 64
                gd[me, r * 64 : r * 64 + 64, b * HALF : b * HALF + LANES] = pair(at, at + 64, 64, True, True)

    pl.run_scoped(
        prepare,
        pltpu.VMEM(view.shape, f32),
        pltpu.VMEM((view.shape[2] // 2 * BLOCK, LANES), f32),
    )
    x_rows(grad_rows, 1).start()
    z_arrival((Q, O), 1)
    y_arrival((Q, O), 0)
    z_arrival((Q, O), 2)
    for k in (I, W, V):
        own_sends_z(k)
    own_sends_y(I)
    y_arrival((Q, O), 1)

    def core_waits(kinds, zz):
        for k in kinds:
            for yy in (y, 1 - y):
                ag_wait(k, zz, yy, 1 - c)

    x_rows_wait(rows_one, 0)

    ends = []
    for p in range(ARTICLES):
        length = 0
        for a in range(ARTICLES):
            length = length + jnp.where(order[0, p] == a, lengths[0, a], 0)
        ends.append(length + ends[-1] if p else length)

    def allowed(first, count):
        ids = lax.broadcasted_iota(jnp.int32, (rows, 1), 0) + first
        start = jnp.zeros((rows, 1), jnp.int32)
        for end in ends:
            start = jnp.where(ids >= end, end, start)
        start = jnp.where(ids >= ends[-1], ids, start)
        keys = lax.broadcasted_iota(jnp.int32, (rows, count), 1)
        return (keys <= ids) & (keys >= start)

    scale = HD ** (-0.5)
    strip = 1024

    def assemble(h):
        for yy in range(2):
            even, odd = gq.at[slot_of(h, yy, 0)], gq.at[slot_of(h, yy, 1)]
            at = yy * 192
            wqkv[h, 0:768, at : at + 64] = even[:, 0:64]
            wqkv[h, 768:1024, at : at + 64] = even[0:256, 64:128]
            wqkv[h, 0:512, at + 64 : at + 128] = even[256:768, 64:128]
            wqkv[h, 512:1024, at + 64 : at + 128] = odd[0:512, 0:64]
            wqkv[h, 0:256, at + 128 : at + 192] = odd[512:768, 0:64]
            wqkv[h, 256:1024, at + 128 : at + 192] = odd[:, 64:128]

    def disassemble(h, value):
        for yy in range(2):
            even, odd = gq.at[slot_of(h, yy, 0)], gq.at[slot_of(h, yy, 1)]
            at = yy * 192
            even[:, 0:64] = value[0:768, at : at + 64]
            even[0:256, 64:128] = value[768:1024, at : at + 64]
            even[256:768, 64:128] = value[0:512, at + 64 : at + 128]
            odd[0:512, 0:64] = value[512:1024, at + 64 : at + 128]
            odd[512:768, 0:64] = value[0:256, at + 128 : at + 192]
            odd[:, 64:128] = value[256:1024, at + 128 : at + 192]

    qv = vecs[pl.ds(6 + t, 1), :]
    for h in range(DEPTH):
        none = jnp.zeros((1, HD), f32)
        qkv_bias[h] = jnp.concatenate([qv[:, h * 256 : h * 256 + 128], none, qv[:, h * 256 + 128 : h * 256 + 256]], 1)

    def head(h):
        core_waits((Q,), h)
        assemble(h)
        qkv[h] = (dot(rows_one[...], wqkv[h]) + qkv_bias[h]).astype(bf)
        for block in range(2):
            at, seen = slice(block * rows, (block + 1) * rows), (block + 1) * rows
            scores = dot_nt(qkv[h, at, 0:128], qkv[h, 0:seen, 128:256]) * scale
            scores = jnp.where(allowed(block * rows, seen), scores, NEG)
            expo = jnp.exp(scores - jnp.max(scores, -1, keepdims=True))
            low = (expo * (1.0 / jnp.sum(expo, -1, keepdims=True))).astype(bf)
            probs[h, at, 0:seen] = low
            ctx[at, lanes(h * HD, HD, HD)] = dot(low, qkv[h, 0:seen, 256:384]).astype(bf)

    head(near(0))
    y_arrival((Q, O), 2)
    z_arrival((Q, O), 3)
    y_arrival((Q, O), 3)
    own_sends_y(W)
    head(near(1))
    own_sends_y(V)
    head(near(2))
    z_arrival((I, W), 1)
    head(near(3))
    y_arrival((I, W), 0)
    for zz in range(DEPTH):
        core_waits((O,), zz)
    def w_out(ref):
        return ref[...].reshape(DEPTH * HD, D)
    far[0] = dot(ctx[other, :], w_out(go)).astype(bf)
    x_part(0).start()
    mixed[...] = tokens[...] + dot(ctx[own, :], w_out(go)) + vecs[4:5, :]
    z_arrival((I, W), 2)
    x_part(0).wait_recv()
    def second_norm(at, step):
        value = mixed[pl.ds(at, step), :] + inx[0, pl.ds(at, step), :].astype(f32)
        mixed[pl.ds(at, step), :] = value
        unit, inverse = norm(value)
        to = pl.ds(pl.multiple_of(t * rows + at, step), step)
        rows_two[to, :] = (unit * vecs[2:3, :] + vecs[3:4, :]).astype(bf)
    x_rows_wait(grad_rows, 1)
    by_rows(second_norm)
    x_rows(rows_two, 2).start()
    v_forward(z, 1 - y)
    macc[...] = jnp.zeros_like(macc)
    y_arrival((I, W), 1)
    nacc[...] = jnp.zeros_like(nacc)
    vout[...] = jnp.zeros_like(vout)
    z_arrival((I, W), 3)
    def ffn(half, zz):
        first = 4 * zz
        at = pl.ds(pl.multiple_of(lax.rem(t + half, 2) * rows, rows), rows)
        units = lanes(zz * 512, 512, 512)
        bias_row = vecs[pl.ds(8 + 2 * t + lax.div(zz, 2), 1), lanes(lax.rem(zz, 2) * 512, 512, 512)]

        def w_in(start, count):
            return jnp.concatenate([gi[first + j, start : start + count, :] for j in range(4)], 1)

        def w_down(start, count):
            return gd[pl.ds(first, 4), :, start : start + count].reshape(512, count)

        inner = dot(rows_two[at, :], w_in(0, D)) + bias_row
        square = inner * inner
        bent = jnp.tanh(GELU_A * inner * (1.0 + GELU_B * square))
        act[at, units] = (0.5 * inner * (1.0 + bent)).astype(bf)
        slope = 0.5 * (1.0 + bent) + 0.5 * inner * (1.0 - bent * bent) * (GELU_A * (1.0 + 3.0 * GELU_B * square))
        gin[at, units] = (dot_nt(grad_rows[at, :], w_down(0, D)) * slope).astype(bf)
        for nb in range(4):
            out = slice(nb * 256, nb * 256 + 256)
            nacc[at, out] += dot_nt(gin[at, units], w_in(nb * 256, 256))
            macc[at, out] += dot(act[at, units], w_down(nb * 256, 256))
    def ffn_grads(zz):
        first = 4 * zz
        units = lanes(zz * 512, 512, 512)
        for k in (I, W, V):
            for yy in range(2):
                drain(k, zz, yy)
        bias_sum[zz] = jnp.sum(gin[:, units].astype(f32), 0, keepdims=True)
        for nb in range(4):
            out = slice(nb * 256, nb * 256 + 256)
            part = dot(rows_t[out, :], gin[:, units]).astype(bf)
            for j in range(4):
                gi[first + j, out, :] = part[:, j * LANES : (j + 1) * LANES]
        for yy in (1 - y, y):
            rc_copy(I, zz, yy).start()
        act_t = act[:, units].T
        for nb in range(4):
            out = slice(nb * 256, nb * 256 + 256)
            part = dot(act_t, grad_rows[:, out]).astype(bf)
            gd[pl.ds(first, 4), :, out] = part.reshape(4, LANES, 256)
        for yy in (1 - y, y):
            rc_copy(W, zz, yy).start()
    def each(kinds, step, *args):
        for k in kinds:
            step(k, *args)
    def reduce_out():
        for yy in (1 - y, y):
            for s in (3, 2, 1, 0):
                rc_add(O, near(s), yy)
    def reduce_head(zz):
        for yy in (1 - y, y):
            rc_add(Q, zz, yy)
    v_arrival(1)
    def reduce_core(zz):
        for yy in (1 - y, y):
            for k in (I, W):
                rc_add(k, zz, yy)
    def v_step(s):
        for yy in (1 - y, y):
            z_step(V, s, yy)
    def v_merge(s):
        for yy in (1 - y, y):
            z_merge(V, s, yy)
    core_waits((I, W, V), z)
    ffn(0, z)
    core_waits((I, W, V), near(1))
    ffn(0, near(1))
    x_rows_wait(rows_two, 2)
    x_out().start()
    v_arrival(2)
    rows_t[...] = rows_two[...].T
    y_arrival((I, W), 2)
    def by_z(s, carry):
        @pl.when(s == 2)
        def _():
            v_arrival(3)
            y_arrival((I, W), 3)

        @pl.when(s >= 2)
        def _():
            core_waits((I, W, V), near(s))
            ffn(0, near(s))

        ffn(1, near(s))

        @pl.when(s == DEPTH - 1)
        def _():
            x_part(0).wait_send()
            far[0] = nacc[other, :].astype(bf)
            x_part(1).start()

        ffn_grads(near(s))

        @pl.when(s > 0)
        def _():
            reduce_core(near(s - 1))

        for before in (1, 2):

            @pl.when(s == before + 1)
            def _():
                v_step(before)

        return carry
    lax.fori_loop(0, DEPTH, by_z, 0)
    x_out().wait_recv()
    reduce_core(near(3))
    x_out_core(c).start()
    v_step(3)
    rows_t[...] = rows_one[...].T
    for zz in range(DEPTH):
        for side in range(2):
            row, start = 8 + 2 * side + zz // 2, zz % 2 * 512
            vout[0, row : row + 1, start : start + 512] = jnp.where(t == side, bias_sum[zz], 0.0)
    v_merge(1)
    x_part(1).wait_recv()
    def row_sum(row, value):
        vout[0, row : row + 1, :] += jnp.sum(value, 0, keepdims=True)
    def second_back(at, step):
        here = pl.ds(at, step)
        in_group = pl.ds(pl.multiple_of(t * rows + at, step), step)
        grad = nacc[in_group, :] + inx[0, here, :].astype(f32)
        unit, inverse = norm(mixed[here, :])
        back = cot[here, :] + norm_grad(grad, unit, inverse, vecs[2:3, :])
        input_grad[here, :] = back
        grad_attn[in_group, :] = back.astype(bf)
        row_sum(2, grad * unit)
        row_sum(3, grad)
        row_sum(4, back)
        row_sum(5, cot[here, :])
    by_rows(second_back)
    early_rows(0)
    x_out_core(1 - c).wait_recv()
    ctx_x[...] = dot_nt(grad_attn[own, :], w_out(go_x)).astype(bf)
    x_grad_context().start()
    gctx[own, :] = dot_nt(grad_attn[own, :], w_out(go)).astype(bf)
    each((I, W), ry_add, 1)
    v_merge(2)
    each((I, W), ry_add, 2)
    for zz in range(DEPTH):
        for yy in range(2):
            drain(O, zz, yy)
            drain(Q, zz, yy)
    def mixed_out(at, step):
        here = pl.ds(at, step)
        in_group = pl.ds(pl.multiple_of(t * rows + at, step), step)
        mixed[here, :] = mixed[here, :] + macc[in_group, :] + inx[1, here, :].astype(f32) + vecs[5:6, :]
    x_out().wait_send()
    x_grad_context_wait()
    far[1] = macc[other, :].astype(bf)
    x_rows(grad_attn, 3).start()
    def out_grads():
        x_rows_wait(grad_attn, 3)
        ctx_t = ctx[...].T
        for nb in range(4):
            at = slice(nb * 256, nb * 256 + 256)
            go[:, :, at] = dot(ctx_t, grad_attn[:, at]).astype(bf).reshape(8, 64, 256)
        for zz in range(DEPTH):
            for yy in range(2):
                rc_copy(O, zz, yy).start()
    def first_back(at, step):
        here = pl.ds(at, step)
        in_group = pl.ds(pl.multiple_of(t * rows + at, step), step)
        grad = nacc[in_group, :] + inx[0, here, :].astype(f32)
        unit, inverse = norm(tokens[here, :])
        input_grad[here, :] = input_grad[here, :] + norm_grad(grad, unit, inverse, vecs[0:1, :])
        row_sum(0, grad * unit)
        row_sum(1, grad)
    def finish_mixed():
        x_part(2).wait_recv()
        by_rows(mixed_out)
    def finish_input():
        x_part(3).wait_recv()
        by_rows(first_back)
    late_rows = (0, 1, 6, 7)
    v_cross()
    def late_start():
        for h in range(DEPTH):
            for row in range(2):
                total = jnp.where(t == row, qv_sum[h], 0.0)
                vout[0, 6 + row : 7 + row, h * 256 : h * 256 + 128] = total[:, 0:128]
                vout[0, 6 + row : 7 + row, h * 256 + 128 : h * 256 + 256] = total[:, 256:384]
        for at, row in enumerate(late_rows):
            for j in range(8):
                late[at * 8 + j : at * 8 + j + 1, :] = vout[0, row : row + 1, j * LANES : (j + 1) * LANES]
        late_in[t * 4 + y * 2 + c] = late[...]
        for turn in range(1, 8):
            late_copy(turn).start()
    def late_cross():
        for turn in range(1, 8):
            late_wait(late_turn(turn)[1])
        total = late_in[0]
        for index in range(1, 8):
            total = total + late_in[index]
        late_sum[...] = total
        late_in[8 + z] = total
        for step in range(1, DEPTH):
            late_z(step).start()
    def vec_finish():
        for step in range(1, DEPTH):
            zz = lax.rem(z + step, DEPTH)
            late_wait(8 + zz)
            remote(vin.at[3 + zz], vin.at[3 + zz], v_send.at[0], v_recv.at[3 + zz], y_peer).wait_recv()
        total = ((late_in[8] + late_in[9]) + late_in[10]) + late_in[11]
        early = ((vin[3] + vin[4]) + vin[5]) + vin[6]
        vec_grads[...] = early[0 : vec_grads.shape[0]]
        for at, row in enumerate(late_rows):
            for j in range(8):
                vec_grads[row : row + 1, j * LANES : (j + 1) * LANES] = total[at * 8 + j : at * 8 + j + 1, :]
    def head_back(h, turn):
        q0, q1 = qkv[h, 0:rows, 0:128], qkv[h, rows : 2 * rows, 0:128]
        grads = []
        for block in range(2):
            at, seen = slice(block * rows, (block + 1) * rows), (block + 1) * rows
            low = probs[h, at, 0:seen]
            given = gctx[at, lanes(h * HD, HD, HD)]
            prob = low.astype(f32)
            grad_probs = dot_nt(given, qkv[h, 0:seen, 256:384])
            delta = jnp.sum(prob * grad_probs, -1, keepdims=True)
            grad_scores = (prob * (grad_probs - delta)).astype(bf)
            grad_q = dot(grad_scores, qkv[h, 0:seen, 128:256]) * scale
            grad_k = dot_tn(grad_scores, q1 if block else q0) * scale
            grad_v = dot_tn(low, given)
            grads.append((grad_q, grad_k, grad_v))
        (gq0, gk0, gv0), (gq1, gk1, gv1) = grads
        top = jnp.concatenate([gq0, gk0 + gk1[0:rows], gv0 + gv1[0:rows]], 1).astype(bf)
        low_half = jnp.concatenate([gq1, gk1[rows:], gv1[rows:]], 1).astype(bf)
        qkv[h, 0:rows, :] = top
        qkv[h, rows : 2 * rows, :] = low_half
        total = jnp.sum(top.astype(f32), 0, keepdims=True) + jnp.sum(low_half.astype(f32), 0, keepdims=True)
        qv_sum[h] = total
        for half in (other, own):
            product = dot_nt(qkv[h, half, :], wqkv[h])
            if turn == 0:
                nacc[half, :] = product
            else:
                nacc[half, :] += product
            if turn == DEPTH - 1 and half is other:
                x_part(1).wait_send()
                far[0] = nacc[other, :].astype(bf)
                x_part(3).start()
        part = dot(rows_t[...], qkv[h]).astype(bf)
        disassemble(h, part)
        for yy in (1 - y, y):
            rc_copy(Q, h, yy).start()
    early_rows(1)
    head_back(near(3), 0)
    early_rows(2)
    head_back(near(2), 1)
    early_rows(3)
    x_part(2).start()
    reduce_head(near(3))
    each((I, W), ry_add, 3)
    each((I, W), ry_merge, 1)
    out_grads()
    reduce_head(near(2))
    head_back(near(1), 2)
    reduce_out()
    each((I, W), ry_merge, 2)
    head_back(z, 3)
    ry_add(Q, 3)
    finish_mixed()
    reduce_head(near(1))
    ry_add(Q, 2)
    ry_add(O, 3)
    ry_add(Q, 1)
    ry_add(O, 2)
    ry_merge(Q, 2)
    reduce_head(z)
    ry_merge(Q, 1)
    ry_add(O, 1)
    own_total(W)
    finish_input()
    late_start()
    ry_merge(O, 2)
    late_cross()
    z_total(V, y, total_of(V), y_landed(V, z))
    ry_merge(O, 1)
    own_total(Q)
    own_total(I)
    vec_finish()
    own_total(O)

    for stage in range(3):
        v_copy(stage).wait_send()
    for turn in range(1, 8):
        late_copy(turn).wait_send()
    for step in range(1, DEPTH):
        vz_copy(step).wait_send()
        late_z(step).wait_send()
    for index, ref in enumerate((rows_one, grad_rows, rows_two, grad_attn)):
        x_rows(ref, index).wait_send()
    for index in (2, 3):
        x_part(index).wait_send()
    x_out_core(c).wait_send()
    x_grad_context().wait_send()
    for k in range(4):
        for zz in range(DEPTH):
            for yy in range(2):
                rc_copy(k, zz, yy).wait_send()
            ry_copy(k, zz).wait_send()
        for s in range(1, DEPTH):
            rz_copy(k, s, y, True).wait_send()
    ry_copy(V, z).wait_send()
    for yy in range(2):
        for s in range(1, DEPTH):
            rz_copy(V, s, yy, True).wait_send()


def run_layer(tokens, cotangent, lengths, order, weights, vec_params):
    bf, f32 = jnp.bfloat16, jnp.float32
    rows = tokens.shape[0]
    group = 2 * rows
    owners = 16
    shapes = piece_shapes()
    view = jnp.transpose(weights, (1, 2, 0))
    there = pl.BlockSpec(memory_space=pl.ANY)
    vmem = pl.BlockSpec(memory_space=pltpu.VMEM)
    smem = pl.BlockSpec(memory_space=pltpu.SMEM)

    halved = shapes[:3] + ((HALF, D),)

    def many(count, kinds):
        return [pltpu.VMEM((count,) + s, bf) for s in kinds]

    full = pltpu.VMEM((group, D), bf)
    dma = pltpu.SemaphoreType.DMA
    return pl.pallas_call(
        layer_kernel,
        out_shape=[jax.ShapeDtypeStruct((rows, D), f32)] * 2
        + [jax.ShapeDtypeStruct(s, f32) for s in shapes]
        + [jax.ShapeDtypeStruct(vec_params.shape, f32)],
        in_specs=[smem, smem, there] + [vmem] * 3,
        out_specs=[vmem] * 7,
        scratch_shapes=[
            pltpu.VMEM((owners,) + shapes[0], bf),
            pltpu.VMEM((owners // 2, BLOCK, D), bf),
            pltpu.VMEM((owners,) + shapes[2], bf),
            pltpu.VMEM((owners,) + shapes[3], bf),
            pltpu.VMEM((DEPTH, D, 3 * HD), bf),
        ]
        + many(2 * DEPTH, shapes)
        + many(DEPTH, halved)
        + many(1, halved[3:])
        + many(DEPTH, halved)
        + many(2 * DEPTH, halved[3:])
        + [
            full,
            full,
            pltpu.VMEM((D, group), bf),
            full,
            full,
            pltpu.VMEM((DEPTH, group, group), bf),
            pltpu.VMEM((DEPTH, group, 3 * HD), bf),
            pltpu.VMEM((group, DEPTH * HD), bf),
            pltpu.VMEM((group, DEPTH * HD), bf),
            pltpu.VMEM((2, rows, D), bf),
            pltpu.VMEM((2, rows, D), bf),
            pltpu.VMEM((owners // 2, BLOCK, D), bf),
            pltpu.VMEM((rows, DEPTH * HD), bf),
            pltpu.VMEM((group, D), f32),
            pltpu.VMEM((group, D), f32),
            pltpu.VMEM((group, 2 * D), bf),
            pltpu.VMEM((group, 2 * D), bf),
            pltpu.VMEM((DEPTH, 1, 512), f32),
            pltpu.VMEM((DEPTH, 1, 3 * HD), f32),
            pltpu.VMEM((DEPTH, 1, 3 * HD), f32),
            pltpu.VMEM((7, 16, D), f32),
            pltpu.VMEM((5, 16, D), f32),
            pltpu.VMEM((32, LANES), f32),
            pltpu.VMEM((32, LANES), f32),
            pltpu.VMEM((12, 32, LANES), f32),
            dma((5, owners)),
            dma((5, DEPTH)),
            dma((5, 2 * DEPTH)),
            dma((5, 2, 2 * DEPTH)),
            dma((4, 2 * DEPTH)),
            dma((4, 2 * DEPTH)),
            dma((5, DEPTH)),
            dma((5, DEPTH)),
            dma((5, 2 * DEPTH)),
            dma((5, 2 * DEPTH)),
            dma((11,)),
            dma((11,)),
            dma((6,)),
            dma((7,)),
            dma((11,)),
            dma((12,)),
            dma((1,)),
        ],
        compiler_params=pltpu.CompilerParams(
            collective_id=0, has_side_effects=True, vmem_limit_bytes=VMEM_LIMIT
        ),
        name="layer",
    )(lengths, order, view, tokens, cotangent, vec_params)


def per_device(
    grp_count,
    tp_count,
    tokens,
    cotangent,
    lengths,
    order,
    weights,
    momentum,
    stat_left,
    stat_right,
    root_left,
    root_right,
    vec_params,
    vec_momentum,
    vec_second,
):
    fits = grp_count == 4 * DEPTH and tp_count == 2 and tokens.shape[0] == 256
    if not fits or lengths.shape[1] != ARTICLES:
        return per_device_general(
            tokens,
            cotangent,
            lengths,
            order,
            weights,
            momentum,
            stat_left,
            stat_right,
            root_left,
            root_right,
            vec_params,
            vec_momentum,
            vec_second,
        )
    token_total = tokens.shape[0] * tp_count * grp_count
    mixed, input_grad, *sums, vec_grads = run_layer(tokens, cotangent, lengths, order, weights, vec_params)
    blocks, vecs, results = update_blocks(
        sums,
        (weights, momentum, stat_left, stat_right, root_left, root_right),
        vec_grads,
        (vec_params, vec_momentum, vec_second),
        (mixed, input_grad),
        token_total,
    )
    return (*results, *blocks, *vecs)


def solution(mesh):
    placed = (
        P(("grp", "tp"), None),
        P(("grp", "tp"), None),
        P("grp", None),
        P("grp", None),
        P(("tp", "grp"), None, None),
        P(("tp", "grp"), None, None),
        P(("tp", "grp"), None, None),
        P(("tp", "grp"), None, None),
        P(("tp", "grp"), None, None),
        P(("tp", "grp"), None, None),
        P(),
        P(),
        P(),
    )
    return jax.shard_map(
        functools.partial(per_device, mesh.shape["grp"], mesh.shape["tp"]),
        mesh=mesh,
        in_specs=placed,
        out_specs=(
            P(("grp", "tp"), None),
            P(("grp", "tp"), None),
            P(("tp", "grp"), None, None),
            P(("tp", "grp"), None, None),
            P(("tp", "grp"), None, None),
            P(("tp", "grp"), None, None),
            P(("tp", "grp"), None, None),
            P(),
            P(),
            P(),
            P(),
        ),
        check_vma=False,
    )
```

profile of v0, /device:TPU:0, one launch (start us, length us, event | category | flops | bytes accessed | tf_op | source)
XLA Modules:
  0.0 180.4 jit_solution(8972406307118058676)
XLA Ops:
  0.6 158.0 %layer.1 = (f32[256,1024]{1,0:T(8,128)}, f32[256,1024]{1,0:T(8,128)}, f32[768,128]{1,0:T(8,128)}, f32[64,512]{1,0:T(8,128)}, f32[1024,128]{1,0:T(8,128)}, /*index=5*/f32[128,1024]{1,0:T(8,128)}, f32[12,1024]{1,0:T(8,128)}) custom-call(s32[1,4]{1,0:T(1,128)} %lengths.1, s32[1,4]{1,0:T(1,128)} %order.1, f32[64,64,96]{2,1,0:T(8,128)} %bitcast.11, ...), custom_call_target="tpu_custom_call" | custom-call | tf_op jit(solution)/shard_map/layer/pallas_call | solution.py:1527
  158.7 21.5 %update_blocks.1 = (f32[64,64,96]{2,1,0:T(8,128)}, f32[64,64,96]{2,1,0:T(8,128)}, f32[64,64,96]{2,1,0:T(8,128)}, f32[64,64,96]{2,1,0:T(8,128)}, f32[64,64,96]{2,...) custom-call(f32[768,128]{1,0:T(8,128)} %get-tuple-element.29.sum_q, ...), custom_call_target="tpu_custom_call" | custom-call | tf_op jit(solution)/shard_map/update_blocks/pallas_call | solution.py:577
where the time goes:
time: 181 us; the launch traced here: 180 us
  Pallas kernels  180 us (99%)
    pallas_call x1, Pallas kernels, run_layer(): pl.pallas_call(layer_kernel, out_shape=[jax.ShapeDtypeStruct((rows, D), f...  158 us
    pallas_call x1, Pallas kernels, update_blocks(): pl.pallas_call(functools.partial(update_kernel, token_total ** (-0.5)), g...  21.5 us

commit v1 on v0

--- a/solution.py
+++ b/solution.py
@@ -385,7 +385,7 @@
     return z * 4 + y * 2 + c
 
 
-def lay_blocks(view_ref, stack):
+def lay_blocks(view_ref, stack, first, last):
     half = view_ref.shape[2] // 2
 
     def row(i, carry):
@@ -393,7 +393,7 @@
         stack[pl.ds(i, half, stride=BLOCK), :] = jnp.concatenate([tile[:half], tile[half:]], 1)
         return carry
 
-    lax.fori_loop(0, BLOCK, row, 0, unroll=8)
+    lax.fori_loop(first, last, row, 0, unroll=8)
 
 
 def piece_shapes():
@@ -408,10 +408,10 @@
 
 def update_kernel(
     scale,
-    sum_q,
-    sum_o,
-    sum_i,
-    sum_d,
+    in_q,
+    in_o,
+    in_i,
+    in_d,
     root_l,
     root_r,
     vec_g,
@@ -444,8 +444,13 @@
     held_m,
     held_sl,
     held_sr,
+    sum_q,
+    sum_o,
+    sum_i,
+    sum_d,
     sems,
     block_sems,
+    sum_sems,
 ):
     count = w.shape[2]
     step_rows = out_w.shape[0]
@@ -471,6 +476,12 @@
         for k in range(4):
             for load in loads(k):
                 load.start()
+        sum_loads = [
+            pltpu.make_async_copy(a, b, sum_sems.at[n])
+            for n, (a, b) in enumerate(((in_q, sum_q), (in_o, sum_o), (in_i, sum_i), (in_d, sum_d)))
+        ]
+        for load in sum_loads:
+            load.start()
         for k in range(BLOCK // step_rows):
             for load in block_loads(k):
                 load.start()
@@ -482,6 +493,17 @@
         momentum = BETA * vec_m[...] + scaled * lax.rsqrt(fresh + VEC_EPS)
         out_vm[...] = momentum
         out_v[...] = vecs[...] - VEC_RATE * momentum
+        def row(i, carry):
+            both = jnp.concatenate([held_l[i], held_r[i]], 0)
+            second[pl.ds(i, count, stride=BLOCK), :] = both.T
+            return carry
+
+        for k in range(4):
+            for load in loads(k):
+                load.wait()
+            lax.fori_loop(16 * k, 16 * k + 16, row, 0, unroll=8)
+        for load in sum_loads:
+            load.wait()
         rows = sum_q.shape[0]
         grads[0:rows, 0:HALF] = sum_q[:, 0:HALF]
         grads[rows : 2 * rows, 0:HALF] = sum_q[:, HALF:LANES]
@@ -496,15 +518,6 @@
                 at = D + (r * 16 + b) * 64
                 grads[at : at + 64, HALF:LANES] = sum_d[r * 64 : r * 64 + 64, b * HALF : (b + 1) * HALF]
 
-        def row(i, carry):
-            both = jnp.concatenate([held_l[i], held_r[i]], 0)
-            second[pl.ds(i, count, stride=BLOCK), :] = both.T
-            return carry
-
-        for k in range(4):
-            for load in loads(k):
-                load.wait()
-            lax.fori_loop(16 * k, 16 * k + 16, row, 0, unroll=8)
         row_id = lax.broadcasted_iota(jnp.int32, (256, 256), 0)
         col_id = lax.broadcasted_iota(jnp.int32, (256, 256), 1)
         mask = lax.shift_right_logical(row_id, 6) == lax.shift_right_logical(col_id, 6)
@@ -567,7 +580,7 @@
 def update_blocks(sums, blocks, vec_grads, vecs, results, token_total):
     views = [jnp.transpose(a, (1, 2, 0)) for a in blocks]
     count = blocks[0].shape[0]
-    rows = 8
+    rows = 16
     whole = pl.BlockSpec(memory_space=pltpu.VMEM)
     steps = BLOCK // rows
     some = pl.BlockSpec((results[0].shape[0] // steps, results[0].shape[1]), lambda i: (i, 0))
@@ -580,15 +593,17 @@
         out_shape=[jax.ShapeDtypeStruct((BLOCK, BLOCK, count), jnp.float32)] * 5
         + [vec] * 4
         + [jax.ShapeDtypeStruct(a.shape, a.dtype) for a in results],
-        in_specs=[whole] * 4 + [there] * 2 + [whole] * 4 + [some] * 2 + [there] * 4,
+        in_specs=[there] * 6 + [whole] * 4 + [some] * 2 + [there] * 4,
         out_specs=[part] * 5 + [whole] * 4 + [some] * 2,
         scratch_shapes=[
             pltpu.VMEM((count // 2 * BLOCK, LANES), jnp.float32),
             pltpu.VMEM((count * BLOCK, LANES), jnp.float32),
             pltpu.VMEM((count * BLOCK, LANES), jnp.float32),
             *[pltpu.VMEM((BLOCK, BLOCK, count), jnp.float32)] * 6,
+            *[pltpu.VMEM(a.shape, a.dtype) for a in sums],
             pltpu.SemaphoreType.DMA((4, 2)),
             pltpu.SemaphoreType.DMA((BLOCK // rows, 4)),
+            pltpu.SemaphoreType.DMA((4,)),
         ],
         compiler_params=pltpu.CompilerParams(vmem_limit_bytes=VMEM_LIMIT),
         name="update_blocks",
@@ -603,16 +618,24 @@
     lengths,
     order,
     view,
+    tokens_in,
+    cot_in,
+    vecs,
+    mixed_there,
+    input_grad_there,
+    out_q,
+    out_o,
+    out_i,
+    out_d,
+    vec_grads,
     tokens,
     cot,
-    vecs,
     mixed,
     input_grad,
     sum_q,
     sum_o,
     sum_i,
     sum_d,
-    vec_grads,
     gq,
     go,
     gi,
@@ -1037,15 +1060,35 @@
         peer = (slot_of(lax.rem(z + step, DEPTH), y, c), t)
         return remote(late_sum, late_in.at[8 + z], l_send.at[7 + step], l_recv.at[8 + z], peer)
 
+    stores = [
+        pltpu.make_async_copy(a, b, copy_sem.at[6 + n])
+        for n, (a, b) in enumerate(
+            (
+                (sum_q, out_q),
+                (sum_o, out_o),
+                (sum_i, out_i),
+                (sum_d, out_d),
+                (mixed, mixed_there),
+                (input_grad, input_grad_there),
+            )
+        )
+    ]
+
     barrier = pltpu.get_barrier_semaphore()
     z_peers = [(slot_of(lax.rem(z + step, DEPTH), y, c), t) for step in range(1, DEPTH)]
     everyone = [late_turn(turn)[0] for turn in range(1, 8)] + z_peers
     for device in everyone:
         pl.semaphore_signal(barrier, inc=1, device_id=device, device_id_type=MESH_ID)
 
+    row_loads = [pltpu.make_async_copy(tokens_in, tokens, copy_sem.at[4]), pltpu.make_async_copy(cot_in, cot, copy_sem.at[5])]
+
     def prepare(held, stack):
-        load = pltpu.make_async_copy(view, held, copy_sem.at[0])
-        load.start()
+        parts = [pl.ds(16 * k, 16) for k in range(4)]
+        loads = [pltpu.make_async_copy(view.at[part], held.at[part], copy_sem.at[k]) for k, part in enumerate(parts)]
+        for load in loads:
+            load.start()
+        for load in row_loads:
+            load.start()
 
         def first_norm(at, step):
             unit, inverse = norm(tokens[pl.ds(at, step), :])
@@ -1053,8 +1096,9 @@
             rows_one[to, :] = (unit * vecs[0:1, :] + vecs[1:2, :]).astype(bf)
             grad_rows[to, :] = cot[pl.ds(at, step), :].astype(bf)
 
-        load.wait()
-        lay_blocks(held, stack)
+        for k, load in enumerate(loads):
+            load.wait()
+            lay_blocks(held, stack, 16 * k, 16 * k + 16)
 
         def pair(left, right, count, left_high=False, right_high=False):
             first, second = stack[left : left + count, :], stack[right : right + count, :]
@@ -1072,6 +1116,8 @@
         for k in (Q, O):
             own_sends_y(k)
             own_sends_z(k)
+        for load in row_loads:
+            load.wait()
         by_rows(first_norm)
         x_rows(rows_one, 0).start()
         base += 512
@@ -1368,9 +1414,11 @@
     def finish_mixed():
         x_part(2).wait_recv()
         by_rows(mixed_out)
+        stores[4].start()
     def finish_input():
         x_part(3).wait_recv()
         by_rows(first_back)
+        stores[5].start()
     late_rows = (0, 1, 6, 7)
     v_cross()
     def late_start():
@@ -1476,10 +1524,14 @@
     z_total(V, y, total_of(V), y_landed(V, z))
     ry_merge(O, 1)
     own_total(Q)
+    stores[Q].start()
     own_total(I)
+    stores[I].start()
     vec_finish()
     own_total(O)
-
+    stores[O].start()
+
+    stores[W].start()
     for stage in range(3):
         v_copy(stage).wait_send()
     for turn in range(1, 8):
@@ -1500,6 +1552,8 @@
             ry_copy(k, zz).wait_send()
         for s in range(1, DEPTH):
             rz_copy(k, s, y, True).wait_send()
+    for store in stores:
+        store.wait()
     ry_copy(V, z).wait_send()
     for yy in range(2):
         for s in range(1, DEPTH):
@@ -1529,9 +1583,11 @@
         out_shape=[jax.ShapeDtypeStruct((rows, D), f32)] * 2
         + [jax.ShapeDtypeStruct(s, f32) for s in shapes]
         + [jax.ShapeDtypeStruct(vec_params.shape, f32)],
-        in_specs=[smem, smem, there] + [vmem] * 3,
-        out_specs=[vmem] * 7,
-        scratch_shapes=[
+        in_specs=[smem, smem] + [there] * 3 + [vmem],
+        out_specs=[there] * 6 + [vmem],
+        scratch_shapes=[pltpu.VMEM((rows, D), f32)] * 4
+        + [pltpu.VMEM(s, f32) for s in shapes]
+        + [
             pltpu.VMEM((owners,) + shapes[0], bf),
             pltpu.VMEM((owners // 2, BLOCK, D), bf),
             pltpu.VMEM((owners,) + shapes[2], bf),
@@ -1585,7 +1641,7 @@
             dma((7,)),
             dma((11,)),
             dma((12,)),
-            dma((1,)),
+            dma((12,)),
         ],
         compiler_params=pltpu.CompilerParams(
             collective_id=0, has_side_effects=True, vmem_limit_bytes=VMEM_LIMIT

time: 181 us -> 176 us (0.972)
  Pallas kernels: 180 us -> 175 us
    pallas_call x1, Pallas kernels: 21.5 us -> 19.1 us  [update_blocks(): pl.pallas_call(functools.partial(update_kernel, token_total ** (-0.5)), g...]
where the time goes in v1:
time: 176 us
  Pallas kernels  175 us (99%)
    pallas_call x1, Pallas kernels, run_layer(): pl.pallas_call(layer_kernel, out_shape=[jax.ShapeDtypeStruct((rows, D), f...  156 us
    pallas_call x1, Pallas kernels, update_blocks(): pl.pallas_call(functools.partial(update_kernel, token_total ** (-0.5)), g...  19.1 us

profile of v1, /device:TPU:0, one launch (start us, length us, event | category | flops | bytes accessed | tf_op | source)
XLA Modules:
  0.0 176.3 jit_solution(16077805034346416964)
XLA Ops:
  0.6 156.3 %layer.1 = (f32[256,1024]{1,0:T(8,128)}, f32[256,1024]{1,0:T(8,128)}, f32[768,128]{1,0:T(8,128)}, f32[64,512]{1,0:T(8,128)}, f32[1024,128]{1,0:T(8,128)}, /*index=5*/f32[128,1024]{1,0:T(8,128)}, f32[12,1024]{1,0:T(8,128)}) custom-call(s32[1,4]{1,0:T(1,128)} %lengths.1, s32[1,4]{1,0:T(1,128)} %order.1, f32[64,64,96]{2,1,0:T(8,128)} %bitcast.11, ...), custom_call_target="tpu_custom_call" | custom-call | tf_op jit(solution)/shard_map/layer/pallas_call | solution.py:1581
  156.9 19.1 %update_blocks.1 = (f32[64,64,96]{2,1,0:T(8,128)}, f32[64,64,96]{2,1,0:T(8,128)}, f32[64,64,96]{2,1,0:T(8,128)}, f32[64,64,96]{2,1,0:T(8,128)}, f32[64,64,96]{2,...) custom-call(f32[768,128]{1,0:T(8,128)} %get-tuple-element.29.in_q, ...), custom_call_target="tpu_custom_call" | custom-call | tf_op jit(solution)/shard_map/update_blocks/pallas_call | solution.py:590

commit v2 on v1

--- a/solution.py
+++ b/solution.py
@@ -994,7 +994,7 @@
             body(pl.multiple_of(i * step, step), step)
             return carry
 
-        lax.fori_loop(0, rows // step, run, 0)
+        lax.fori_loop(0, rows // step, run, 0, unroll=2)
 
     def norm(value):
         average = jnp.mean(value, -1, keepdims=True)
@@ -1165,7 +1165,6 @@
         return (keys <= ids) & (keys >= start)
 
     scale = HD ** (-0.5)
-    strip = 1024
 
     def assemble(h):
         for yy in range(2):

time: 176 us -> 176 us (level)
  no operation moved by 1% of the time
where the time goes in v2:
time: 176 us
  Pallas kernels  175 us (99%)
    pallas_call x1, Pallas kernels, run_layer(): pl.pallas_call(layer_kernel, out_shape=[jax.ShapeDtypeStruct((rows, D), f...  156 us
    pallas_call x1, Pallas kernels, update_blocks(): pl.pallas_call(functools.partial(update_kernel, token_total ** (-0.5)), g...  19.1 us

profile of v2, /device:TPU:0, one launch (start us, length us, event | category | flops | bytes accessed | tf_op | source)
XLA Modules:
  0.0 175.6 jit_solution(14944219550010544077)
XLA Ops:
  0.6 155.6 %layer.1 = (f32[256,1024]{1,0:T(8,128)}, f32[256,1024]{1,0:T(8,128)}, f32[768,128]{1,0:T(8,128)}, f32[64,512]{1,0:T(8,128)}, f32[1024,128]{1,0:T(8,128)}, /*index=5*/f32[128,1024]{1,0:T(8,128)}, f32[12,1024]{1,0:T(8,128)}) custom-call(s32[1,4]{1,0:T(1,128)} %lengths.1, s32[1,4]{1,0:T(1,128)} %order.1, f32[64,64,96]{2,1,0:T(8,128)} %bitcast.11, ...), custom_call_target="tpu_custom_call" | custom-call | tf_op jit(solution)/shard_map/layer/pallas_call | solution.py:1580
  156.3 19.1 %update_blocks.1 = (f32[64,64,96]{2,1,0:T(8,128)}, f32[64,64,96]{2,1,0:T(8,128)}, f32[64,64,96]{2,1,0:T(8,128)}, f32[64,64,96]{2,1,0:T(8,128)}, f32[64,64,96]{2,...) custom-call(f32[768,128]{1,0:T(8,128)} %get-tuple-element.29.in_q, ...), custom_call_target="tpu_custom_call" | custom-call | tf_op jit(solution)/shard_map/update_blocks/pallas_call | solution.py:590
